TPU v7x, 256 devices: a whole 4x4x8 slice. The times are simulated.
256 devices in a mesh: leaf: 256 (over z, x, y, core).
Axes of the slice: x: 4, y: 4, z: 8, core: 2. Of those that a mesh axis runs over, the one named last changes fastest.
Arguments:
- vectors: float32 [64, 262144], P(None, 'leaf'), may hold values from -6 to 6
- points: float32 [3, 262144], P(None, 'leaf'), may hold values from 0 to 1
- noise: float32 [262144], P('leaf'), may hold values from 0.05 to 1
- bases: float32 [256, 262144], P(None, 'leaf'), may hold values from -0.375 to 0.375
- transfer: float32 [2, 256, 256], replicated, may hold values from -0.25 to 0.25
- proxies: float32 [3, 256], replicated, may hold values from -3.504 to 3.504
- near_src: int32 [1024, 8], P('leaf'), may hold values from 0 to 1023, as said below
- near_count: int32 [1024], P('leaf'), may hold values from 1 to 8
- far_flags: int32 [1792, 3], P('leaf'), may hold values 0 or 1
Outputs:
- product: float32 [64, 262144], P(None, 'leaf')
Inputs may be any that keep to these rules, and one draw needn't show every extreme that they name: `near_src`: row n's entries lie within 4 of n; slot 0, and every slot at or past near_count[n], holds n itself.
All inputs are finite; a program needn't handle non-finite values. No bound on the sum of `far_flags` on one device may be relied on, other than what follows from the above.
Results may differ from a plain program's by a relative error of at most 0.0003.
Values sent between devices are 32-bit elements; how exact they have to be, the bound alone decides.
A program may use at most 64 MiB of HBM per device.

v0:
```python
import functools
import math

import jax
import jax.numpy as jnp
from jax import lax
from jax.experimental import pallas as pl
from jax.experimental.pallas import tpu as pltpu
from jax.sharding import PartitionSpec as P

SHORT_SCALE = 0.02
LONG_SCALE = 1.0
ROOT_THREE = 1.7320508075688772
LOG2_E = 1.4426950408889634

F32 = jnp.float32
BF16 = jnp.bfloat16
MESH = pl.DeviceIdType.MESH

LEAVES = 4
LEAF = 256
RANK = 256
RHS = 64
ROWS = 2
PLANE = 32
PLANES = 8
DEVICES = PLANE * PLANES
TOP = 10
HALO = 3
CHUNK = 32

NORMAL = (((1,), (0,)), ((), ()))
TRANSPOSED = (((1,), (1,)), ((), ()))

PLANE_LEVELS = (2, 3, 4, 5, 6)

SEM_A, SEM_TOP, SEM_B = 0, 1, 2
SEM_VEC, SEM_PTS, SEM_RIM0, SEM_RIM1, SEM_EDGE = 3, 5, 7, 9, 11
SEMS = SEM_EDGE + 2 * len(PLANE_LEVELS)


def nodes_at(level):
    return PLANE >> (level - 2)


def reversed_bits(value, count):
    result = 0
    for bit in range(count):
        result = result * 2 + (value >> bit & 1)
    return result


def halves(x):
    head = x.astype(BF16).astype(F32)
    return jnp.concatenate([head, x - head], axis=0).astype(BF16)


def head_and_rest(x):
    head = x.astype(BF16)
    return head, (x - head.astype(F32)).astype(BF16)


def mul(stacked, w_head, w_rest, dims=NORMAL):
    rows = stacked.shape[0] // 2
    if rows % 16 == 0:
        first = lax.dot_general(stacked, w_head, dims, preferred_element_type=F32)
        second = lax.dot_general(stacked[:rows], w_rest, dims, preferred_element_type=F32)
        return first[:rows] + first[rows:] + second
    both = lax.dot_general(stacked, w_head, dims, preferred_element_type=F32)
    both = both + lax.dot_general(stacked, w_rest, dims, preferred_element_type=F32)
    return both[:rows] + both[rows:]


def stack(first, second, rows):
    if rows % 8 == 0:
        return jnp.concatenate([first[:rows], second[:rows]], axis=0)
    place = lax.broadcasted_iota(jnp.int32, first.shape, 0)
    return jnp.where(place < rows, first, pltpu.roll(second, rows, 0))


def second_half(x, rows):
    if rows % 8 == 0:
        return x[rows:]
    return pltpu.roll(x, x.shape[0] - rows, 0)


def kernel(
    vec,
    pts,
    noise,
    bases,
    transfer,
    prox,
    src,
    cnt,
    flags,
    out,
    vhl,
    bh,
    bl,
    th,
    tl,
    vside,
    ppad,
    pside,
    cols,
    kh,
    kl,
    ch,
    cl,
    near,
    ex0,
    ex1,
    f0,
    f1,
    sa,
    sb,
    rb,
    s7,
    e2,
    e3,
    e4,
    e5,
    e6,
    top7,
    top8,
    gm,
    gp,
    ge,
    go,
    gf,
    g2,
    fs,
    send,
    recv,
):
    edge_of = {2: e2, 3: e3, 4: e4, 5: e5, 6: e6}
    me = lax.axis_index("leaf")
    z, j = me // PLANE, me % PLANE
    left = (me + DEVICES - 1) % DEVICES
    right = (me + 1) % DEVICES
    below = (me + DEVICES - PLANE) % DEVICES
    above = (me + PLANE) % DEVICES

    barrier = pltpu.get_barrier_semaphore()

    def greet(device):
        pl.semaphore_signal(barrier, inc=1, device_id=(device,), device_id_type=MESH)

    @pl.loop(1, PLANE)
    def _(step):
        greet(z * PLANE + (j + step) % PLANE)

    @pl.loop(1, PLANES)
    def _(step):
        greet((z + step) % PLANES * PLANE + j)

    greet(left)
    greet(right)

    def copy(source, target, sem, device):
        return pltpu.make_async_remote_copy(
            src_ref=source,
            dst_ref=target,
            send_sem=send.at[sem],
            recv_sem=recv.at[sem],
            device_id=(device,),
            device_id_type=MESH,
        )

    head, rest = head_and_rest(transfer[...].reshape(2 * RANK, RANK))
    th[...] = head
    tl[...] = rest
    coef0 = []
    for leaf in range(LEAVES):
        lanes = slice(leaf * LEAF, (leaf + 1) * LEAF)
        head, rest = head_and_rest(bases[:, lanes])
        bh[:, lanes] = head
        bl[:, lanes] = rest
        pair = halves(vec[:, lanes])
        vhl[4 + leaf] = pair
        value = mul(pair, head, rest, TRANSPOSED)
        ex0[2 + leaf] = value
        coef0.append(value)

    def parents(children):
        return mul(halves(children), th[...], tl[...])

    pair_rows = [jnp.concatenate([coef0[2 * n], coef0[2 * n + 1]], axis=1) for n in range(2)]
    coef1 = parents(jnp.concatenate(pair_rows, axis=0))
    ex1[2] = coef1[:RHS]
    ex1[3] = coef1[RHS:]
    coef2 = parents(jnp.concatenate([coef1[:RHS], coef1[RHS:]], axis=1))

    lane = lax.broadcasted_iota(jnp.int32, (ROWS, 128), 1)
    root_flags = jnp.zeros((ROWS, 128), F32)
    for which in range(3):
        root_flags = jnp.where(lane == which, flags[6, which].astype(F32), root_flags)
    g2[...] = coef2
    for i in range(PLANE):
        sa[i, :, 0:RANK] = g2[ROWS * i : ROWS * (i + 1), :]
        sa[i, :, RANK:] = root_flags

    pl.semaphore_wait(barrier, PLANE - 1 + PLANES - 1 + 2)

    @pl.loop(1, PLANE)
    def _(step):
        other = (j + step) % PLANE
        copy(sa.at[other], e2.at[HALO + j], SEM_A, z * PLANE + other).start()

    e2[HALO + j] = sa[j]

    ppad[...] = jnp.zeros_like(ppad)
    ppad[0:3, :] = pts[...]
    side_copies = [
        copy(ppad, pside.at[0], SEM_PTS, right),
        copy(ppad, pside.at[1], SEM_PTS + 1, left),
        copy(vec, vside.at[0], SEM_VEC, right),
        copy(vec, vside.at[1], SEM_VEC + 1, left),
        copy(ex0.at[pl.ds(4, 2)], ex0.at[pl.ds(0, 2)], SEM_RIM0, right),
        copy(ex0.at[pl.ds(2, 2)], ex0.at[pl.ds(6, 2)], SEM_RIM0 + 1, left),
        copy(ex1.at[pl.ds(2, 2)], ex1.at[pl.ds(0, 2)], SEM_RIM1, right),
        copy(ex1.at[pl.ds(2, 2)], ex1.at[pl.ds(4, 2)], SEM_RIM1 + 1, left),
    ]
    for item in side_copies:
        item.start()

    prox_rows = prox[...]
    prox_cols = jnp.concatenate([prox_rows, jnp.zeros((5, RANK), F32)], axis=0).T
    gf[...] = prox_cols

    for axis in range(3):
        side = 2.0 ** ((axis - TOP) / 3.0)
        for place, offset in enumerate((2.0, 3.0)):

            @pl.loop(0, RANK // CHUNK)
            def _(step):
                rows = pl.ds(step * CHUNK, CHUNK)
                squared = None
                for c in range(3):
                    column = gf[rows, c : c + 1]
                    if c == axis:
                        column = column - offset
                    delta = column - prox_rows[c : c + 1, :]
                    squared = delta * delta if squared is None else squared + delta * delta
                distance = squared * lax.rsqrt(jnp.maximum(squared, 1e-30))
                u = distance * (ROOT_THREE / SHORT_SCALE * side)
                v = distance * (ROOT_THREE / LONG_SCALE * side)
                eu = jnp.exp2(u * -LOG2_E)
                ev = jnp.exp2(v * -LOG2_E)
                for third in range(3):
                    value = (1.0 + u) * eu + (1.0 + v) * ev
                    head, rest = head_and_rest(value)
                    at = 2 * (axis + 3 * third) + place
                    ch[at, rows, :] = head
                    cl[at, rows, :] = rest
                    if third < 2:
                        u, v, eu, ev = u + u, v + v, eu * eu, ev * ev

    def field(level, minus, plus, even, odd, rows):
        two, three = 2 * level, 2 * level + 1
        first = mul(halves(minus), ch[two], cl[two])
        second = mul(halves(plus), ch[two], cl[two], TRANSPOSED)
        even_part = mul(halves(even), ch[three], cl[three], TRANSPOSED)
        odd_part = mul(halves(odd), ch[three], cl[three])
        if rows is None:
            return first, second, even_part, odd_part
        return (first + second + stack(even_part, odd_part, rows)) * (1.0 / 32.0)

    gm[...] = jnp.zeros_like(gm)
    gp[...] = jnp.zeros_like(gp)
    ge[...] = jnp.zeros_like(ge)
    go[...] = jnp.zeros_like(go)

    def columns_of(window, points):
        cols[window] = points.T

    def evaluate(reader, window, slot):
        reader_rows = ppad[:, pl.ds(pl.multiple_of(reader * LEAF, LEAF), LEAF)]

        @pl.loop(0, LEAF // CHUNK)
        def _(step):
            rows = pl.ds(step * CHUNK, CHUNK)
            squared = None
            for c in range(3):
                delta = cols[window, rows, c : c + 1] - reader_rows[c : c + 1, :]
                squared = delta * delta if squared is None else squared + delta * delta
            distance = squared * lax.rsqrt(jnp.maximum(squared, 1e-30))
            u = distance * (ROOT_THREE / SHORT_SCALE)
            v = distance * (ROOT_THREE / LONG_SCALE)
            value = (1.0 + u) * jnp.exp2(u * -LOG2_E) + (1.0 + v) * jnp.exp2(v * -LOG2_E)
            head, rest = head_and_rest(value)
            kh[slot, rows, :] = head
            kl[slot, rows, :] = rest

    def amount(reader, window):
        target = me * LEAVES + window - 4
        total = jnp.float32(0.0)
        for slot in range(8):
            hit = jnp.logical_and(slot < cnt[reader], src[reader, slot] == target)
            total = total + jnp.where(hit, 1.0, 0.0)
        return total

    def gather_near(reader, window, slot, dims):
        near[reader] += amount(reader, window) * mul(vhl[window], kh[slot], kl[slot], dims)

    near[...] = jnp.zeros_like(near)
    for leaf in range(LEAVES):
        columns_of(4 + leaf, ppad[:, leaf * LEAF : (leaf + 1) * LEAF])

    @pl.loop(0, LEAVES)
    def _(leaf):
        evaluate(leaf, 4 + leaf, 0)
        gather_near(leaf, 4 + leaf, 0, NORMAL)

    copy(sa.at[pl.ds(0, PLANE - 1)], e2.at[pl.ds(HALO, PLANE - 1)], SEM_A, left).wait_recv()
    edge_copies = []

    def send_edges(level):
        ref, nodes = edge_of[level], nodes_at(level)
        width = min(HALO, nodes)
        at = SEM_EDGE + 2 * (level - 2)
        for item in (
            copy(
                ref.at[pl.ds(HALO + nodes - width, width)],
                ref.at[pl.ds(HALO - width, width)],
                at,
                above,
            ),
            copy(ref.at[pl.ds(HALO, width)], ref.at[pl.ds(HALO + nodes, width)], at + 1, below),
        ):
            item.start()
            edge_copies.append(item)

    send_edges(2)
    for p in range(PLANE):
        g2[ROWS * p : ROWS * (p + 1), :] = e2[HALO + reversed_bits(p, 5), :, 0:RANK]
    current = g2[...]
    for level in (3, 4, 5, 6, 7):
        rows = ROWS * nodes_at(level)
        both = jnp.concatenate([current[: max(rows, 8)], second_half(current, rows)], axis=1)
        current = parents(both)
        if level < 7:
            count = 7 - level
            for p in range(nodes_at(level)):
                edge_of[level][HALO + reversed_bits(p, count)] = current[ROWS * p : ROWS * (p + 1)]
            send_edges(level)
    s7[...] = current[0:ROWS]

    @pl.loop(1, PLANES)
    def _(step):
        other = (z + step) % PLANES
        copy(s7, top7.at[HALO + z], SEM_TOP, other * PLANE + j).start()

    top7[HALO + z] = s7[...]
    top7[0:HALO] = jnp.zeros((HALO, ROWS, RANK), F32)
    top7[HALO + PLANES :] = jnp.zeros((HALO, ROWS, RANK), F32)
    top8[...] = jnp.zeros_like(top8)

    inside_below = jnp.where(z > 0, 1.0, 0.0)
    inside_above = jnp.where(z < PLANES - 1, 1.0, 0.0)
    for item in edge_copies:
        item.wait_recv()

    def plane_field(level):
        ref, nodes = edge_of[level], nodes_at(level)
        count = 7 - level

        def at(node):
            value = ref[HALO + node, :, 0:RANK]
            if node < 0:
                value = value * inside_below
            if node >= nodes:
                value = value * inside_above
            return value

        for p in range(nodes):
            node = reversed_bits(p, count)
            rows = slice(ROWS * p, ROWS * (p + 1))
            gm[rows, :] = at(node - 2)
            gp[rows, :] = at(node + 2)
            if p < nodes // 2:
                ge[rows, :] = at(node + 3)
            else:
                half = p - nodes // 2
                go[ROWS * half : ROWS * (half + 1), :] = at(node - 3)
            if level == 2:
                gf[rows, :] = ref[HALO + node, :, RANK : RANK + 8]
        size = max(ROWS * nodes, 8)
        half_size = max(ROWS * nodes // 2, 8)
        minus, plus = gm[0:size, :], gp[0:size, :]
        even, odd = ge[0:half_size, :], go[0:half_size, :]
        if level == 2:
            weights = gf[0:size, :]
            minus = minus * weights[:, 0:1]
            plus = plus * weights[:, 1:2]
            even = even * weights[:half_size, 2:3]
            odd = odd * weights[half_size:, 2:3]
        fs[level - 2, 0:size, :] = field(level, minus, plus, even, odd, ROWS * nodes // 2)

    for level in PLANE_LEVELS:
        plane_field(level)

    copy(
        top7.at[pl.ds(HALO, PLANES - 1)], top7.at[pl.ds(HALO, PLANES - 1)], SEM_TOP, left
    ).wait_recv()
    for p in range(PLANES):
        g2[ROWS * p : ROWS * (p + 1), :] = top7[HALO + reversed_bits(p, 3)]
    coef8 = parents(jnp.concatenate([g2[0:8, :], g2[8:16, :]], axis=1))
    for p in range(4):
        top8[HALO + reversed_bits(p, 2)] = coef8[ROWS * p : ROWS * (p + 1)]

    def own_field(level, ref, node):
        parity = node % 2
        gm[0:ROWS, :] = ref[HALO + node - 2]
        gp[0:ROWS, :] = ref[HALO + node + 2]
        ge[0:ROWS, :] = ref[jnp.where(parity == 0, HALO + node + 3, HALO + node - 3)]
        third = ge[0:8, :]
        first, second, even, odd = field(level, gm[0:8, :], gp[0:8, :], third, third, None)
        return (first + second + jnp.where(parity == 0, even, odd)) * (1.0 / 32.0)

    def children(parent):
        return mul(halves(parent), th[...], tl[...], TRANSPOSED)

    field7 = own_field(7, top7, z)
    down = own_field(8, top8, z // 2)
    both = children(down)
    down = field7 + jnp.where(z % 2 == 0, both[:, :RANK], both[:, RANK:])
    for level in (6, 5, 4, 3, 2):
        size = max(ROWS * nodes_at(level), 8)
        both = children(down)
        rows = ROWS * nodes_at(level) // 2
        down = fs[level - 2, 0:size, :] + stack(both[:, :RANK], both[:, RANK:], rows)
    for p in range(PLANE):
        sb[reversed_bits(p, 5)] = down[ROWS * p : ROWS * (p + 1)]

    @pl.loop(1, PLANE)
    def _(step):
        other = (j + step) % PLANE
        copy(sb.at[other], rb.at[j], SEM_B, z * PLANE + other).start()

    rb[j] = sb[j]

    for item in side_copies:
        item.wait_recv()
    has_left = jnp.where(me > 0, 1.0, 0.0)
    has_right = jnp.where(me < DEVICES - 1, 1.0, 0.0)

    def local_field(level, ref, nodes, first_row, target):
        def at(node, which, reader):
            weight = flags[first_row + reader, which].astype(F32)
            if node < 0:
                weight = weight * has_left
            if node >= nodes:
                weight = weight * has_right
            return ref[2 + node] * weight

        order = list(range(0, nodes, 2)) + list(range(1, nodes, 2))
        minus = jnp.concatenate([at(n - 2, 0, n) for n in order], axis=0)
        plus = jnp.concatenate([at(n + 2, 1, n) for n in order], axis=0)
        even = jnp.concatenate([at(n + 3, 2, n) for n in range(0, nodes, 2)], axis=0)
        odd = jnp.concatenate([at(n - 3, 2, n) for n in range(1, nodes, 2)], axis=0)
        value = field(level, minus, plus, even, odd, RHS * nodes // 2)
        for place, n in enumerate(order):
            target[n] = value[RHS * place : RHS * (place + 1)]

    local_field(0, ex0, LEAVES, 0, f0)
    local_field(1, ex1, LEAVES // 2, LEAVES, f1)

    for leaf in range(LEAVES):
        lanes = slice(leaf * LEAF, (leaf + 1) * LEAF)
        vhl[leaf] = halves(vside[0, :, lanes])
        vhl[8 + leaf] = halves(vside[1, :, lanes])
        columns_of(leaf, pside[0, :, lanes])
        columns_of(8 + leaf, pside[1, :, lanes])

    for first in range(LEAVES):
        for second in range(first + 1, LEAVES):
            evaluate(first, 4 + second, 0)
            gather_near(first, 4 + second, 0, NORMAL)
            gather_near(second, 4 + first, 0, TRANSPOSED)

    @pl.loop(0, 5 * LEAVES)
    def _(index):
        reader = index // 5
        step = index % 5
        window = reader + step + jnp.where(step < 4 - reader, 0, 4)
        evaluate(reader, window, 0)
        gather_near(reader, window, 0, NORMAL)

    copy(sb.at[pl.ds(0, PLANE - 1)], rb.at[pl.ds(0, PLANE - 1)], SEM_B, left).wait_recv()
    for i in range(PLANE):
        g2[ROWS * i : ROWS * (i + 1), :] = rb[i]
    both = children(g2[...])
    down1 = jnp.concatenate([f1[0] + both[:, :RANK], f1[1] + both[:, RANK:]], axis=0)
    both = children(down1)
    for leaf in range(LEAVES):
        lanes = slice(leaf * LEAF, (leaf + 1) * LEAF)
        part = both[RHS * (leaf // 2) : RHS * (leaf // 2 + 1)]
        part = part[:, RANK * (leaf % 2) : RANK * (leaf % 2 + 1)]
        far = mul(halves(f0[leaf] + part), bh[:, lanes], bl[:, lanes])
        own = noise[:, lanes] * vec[:, lanes]
        out[:, lanes] = own + far + near[leaf] * (1.0 / 32.0)

    copy(sa.at[pl.ds(0, PLANE - 1)], e2.at[pl.ds(HALO, PLANE - 1)], SEM_A, left).wait_send()
    copy(sb.at[pl.ds(0, PLANE - 1)], rb.at[pl.ds(0, PLANE - 1)], SEM_B, left).wait_send()
    copy(
        top7.at[pl.ds(HALO, PLANES - 1)], top7.at[pl.ds(HALO, PLANES - 1)], SEM_TOP, left
    ).wait_send()
    for item in side_copies + edge_copies:
        item.wait_send()


def on_device(vectors, points, noise, bases, transfer, proxies, near_src, near_count, far_flags):
    vmem = pl.BlockSpec(memory_space=pltpu.VMEM)
    smem = pl.BlockSpec(memory_space=pltpu.SMEM)
    width = RANK + 128

    def buffer(*shape, dtype=F32):
        return pltpu.VMEM(shape, dtype)

    scratch = [
        buffer(12, 2 * RHS, LEAF, dtype=BF16),
        buffer(RANK, LEAVES * LEAF, dtype=BF16),
        buffer(RANK, LEAVES * LEAF, dtype=BF16),
        buffer(2 * RANK, RANK, dtype=BF16),
        buffer(2 * RANK, RANK, dtype=BF16),
        buffer(2, RHS, LEAVES * LEAF),
        buffer(8, LEAVES * LEAF),
        buffer(2, 8, LEAVES * LEAF),
        buffer(12, LEAF, 8),
        buffer(2, LEAF, LEAF, dtype=BF16),
        buffer(2, LEAF, LEAF, dtype=BF16),
        buffer(18, RANK, RANK, dtype=BF16),
        buffer(18, RANK, RANK, dtype=BF16),
        buffer(LEAVES, RHS, LEAF),
        buffer(LEAVES + 4, RHS, RANK),
        buffer(LEAVES // 2 + 4, RHS, RANK),
        buffer(LEAVES, RHS, RANK),
        buffer(LEAVES // 2, RHS, RANK),
        buffer(PLANE, ROWS, width),
        buffer(PLANE, ROWS, RANK),
        buffer(PLANE, ROWS, RANK),
        buffer(ROWS, RANK),
        buffer(PLANE + 2 * HALO, ROWS, width),
    ]
    for level in PLANE_LEVELS[1:]:
        scratch.append(buffer(nodes_at(level) + 2 * HALO, ROWS, RANK))
    scratch += [
        buffer(PLANES + 2 * HALO, ROWS, RANK),
        buffer(4 + 2 * HALO, ROWS, RANK),
        buffer(RHS, RANK),
        buffer(RHS, RANK),
        buffer(RHS, RANK),
        buffer(RHS, RANK),
        buffer(RANK, 8),
        buffer(RHS, RANK),
        buffer(len(PLANE_LEVELS), RHS, RANK),
        pltpu.SemaphoreType.DMA((SEMS,)),
        pltpu.SemaphoreType.DMA((SEMS,)),
    ]
    return pl.pallas_call(
        kernel,
        out_shape=jax.ShapeDtypeStruct(vectors.shape, F32),
        in_specs=[vmem] * 6 + [smem] * 3,
        out_specs=vmem,
        scratch_shapes=scratch,
        compiler_params=pltpu.CompilerParams(
            collective_id=0, has_side_effects=True, vmem_limit_bytes=48 * 2**20
        ),
        cost_estimate=pl.CostEstimate(
            flops=3 * 10**9, bytes_accessed=3 * 10**6, transcendentals=10**7
        ),
    )(
        vectors,
        points,
        noise.reshape(1, -1),
        bases,
        transfer,
        proxies,
        near_src,
        near_count,
        far_flags,
    )


def solution(mesh):
    in_specs = (
        P(None, "leaf"),
        P(None, "leaf"),
        P("leaf"),
        P(None, "leaf"),
        P(),
        P(),
        P("leaf", None),
        P("leaf"),
        P("leaf", None),
    )
    return jax.shard_map(
        on_device, mesh=mesh, in_specs=in_specs, out_specs=P(None, "leaf"), check_vma=False
    )
```

profile of v0, /device:TPU:1, one launch (start us, length us, event | category | flops | bytes accessed | tf_op | source)
XLA Modules:
  0.0 68.3 jit_solution(5562121160801656641)
XLA Ops:
  0.0 0.0 copy-start.4
  0.0 0.0 copy-start.6
  0.0 0.0 copy-start.7
  0.0 0.8 %copy.10.flags = s32[7,3]{1,0:T(8,128)S(1)} copy(s32[7,3]{0,1:T(4,128)} %param.17) | data formatting | bytes 168 | tf_op args[8]
  0.8 0.0 copy-done.4
  0.8 0.0 copy-done.6
  0.8 0.0 copy-done.7
  0.8 0.0 copy-start
  0.8 1.2 %copy-done = f32[256,1024]{1,0:T(8,128)S(1)} copy-done((f32[256,1024]{1,0:T(8,128)S(1)}, f32[256,1024]{1,0:T(8,128)}, u32[]{:S(2)}) %copy-start) | copy-done | bytes 1048600
  2.0 0.0 copy-start.1
  2.1 1.0 %copy-done.1 = f32[2,256,256]{2,1,0:T(8,128)S(1)} copy-done((f32[2,256,256]{2,1,0:T(8,128)S(1)}, f32[2,256,256]{2,1,0:T(8,128)}, u32[]{:S(2)}) %copy-start.1) | copy-done | bytes 524312
  3.1 0.0 copy-start.2
  3.1 0.9 %copy-done.2 = f32[64,1024]{1,0:T(8,128)S(1)} copy-done((f32[64,1024]{1,0:T(8,128)S(1)}, f32[64,1024]{1,0:T(8,128)}, u32[]{:S(2)}) %copy-start.2) | copy-done | bytes 262168
  4.0 0.0 copy-start.3
  4.0 0.7 %copy-done.3 = f32[3,1024]{1,0:T(4,128)S(1)} copy-done((f32[3,1024]{1,0:T(4,128)S(1)}, f32[3,1024]{1,0:T(4,128)}, u32[]{:S(2)}) %copy-start.3) | copy-done | bytes 12312
  4.8 0.0 copy-start.5
  4.8 0.7 %copy-done.5 = f32[3,256]{1,0:T(4,128)S(1)} copy-done((f32[3,256]{1,0:T(4,128)S(1)}, f32[3,256]{1,0:T(4,128)}, u32[]{:S(2)}) %copy-start.5) | copy-done | bytes 3096
  5.4 62.2 %shard_map.91 = f32[64,1024]{1,0:T(8,128)S(1)} custom-call(f32[64,1024]{1,0:T(8,128)S(1)} %copy-done.2, f32[3,1024]{1,0:T(4,128)S(1)} %copy-done.3, f32[1,1024]{1,0:T(1,128)S(1)} %bitcast.1, f32[256,1024]{1,0:T(8,128)S(1)} %copy-done, f32[2,256,256]{2,1,0:T(8,128)S(1)} %copy-done.1, f32[3,256]{1,0:T(4,128)S(1)} %copy-done.5, s32[4,8]{1,0:T(4,128)S(1)} %copy-done.6, ...), custom_call_target="tpu_custom_call" | custom-call | flops 3000000000 | bytes 3000000 | tf_op jit(solution)/shard_map/pallas_call | solution.py:562
  67.6 0.7 %copy.12 = f32[64,1024]{1,0:T(8,128)} copy(f32[64,1024]{1,0:T(8,128)S(1)} %shard_map.91) | data formatting | bytes 524288
Async XLA Ops:
  0.0 0.8 %copy-start.4 = (f32[1024]{0:T(1024)S(1)}, f32[1024]{0:T(1024)}, u32[]{:S(2)}) copy-start(f32[1024]{0:T(1024)} %param.11) | copy-start | bytes 12292
  0.0 0.8 %copy-start.6 = (s32[4,8]{1,0:T(4,128)S(1)}, s32[4,8]{1,0:T(4,128)}, u32[]{:S(2)}) copy-start(s32[4,8]{1,0:T(4,128)} %src.1) | copy-start | bytes 388
  0.0 0.8 %copy-start.7 = (s32[4]{0:T(128)S(1)}, s32[4]{0:T(128)}, u32[]{:S(2)}) copy-start(s32[4]{0:T(128)} %cnt.1) | copy-start | bytes 52
  0.8 1.2 %copy-start = (f32[256,1024]{1,0:T(8,128)S(1)}, f32[256,1024]{1,0:T(8,128)}, u32[]{:S(2)}) copy-start(f32[256,1024]{1,0:T(8,128)} %bases.1) | copy-start | bytes 3145732
  2.0 1.0 %copy-start.1 = (f32[2,256,256]{2,1,0:T(8,128)S(1)}, f32[2,256,256]{2,1,0:T(8,128)}, u32[]{:S(2)}) copy-start(f32[2,256,256]{2,1,0:T(8,128)} %transfer.1) | copy-start | bytes 1572868
  3.1 0.9 %copy-start.2 = (f32[64,1024]{1,0:T(8,128)S(1)}, f32[64,1024]{1,0:T(8,128)}, u32[]{:S(2)}) copy-start(f32[64,1024]{1,0:T(8,128)} %vec.1) | copy-start | bytes 786436
  4.0 0.7 %copy-start.3 = (f32[3,1024]{1,0:T(4,128)S(1)}, f32[3,1024]{1,0:T(4,128)}, u32[]{:S(2)}) copy-start(f32[3,1024]{1,0:T(4,128)} %pts.1) | copy-start | bytes 36868
  4.8 0.7 %copy-start.5 = (f32[3,256]{1,0:T(4,128)S(1)}, f32[3,256]{1,0:T(4,128)}, u32[]{:S(2)}) copy-start(f32[3,256]{1,0:T(4,128)} %prox.1) | copy-start | bytes 9220
where the time goes:
time: 68.7 us; the launch traced here: 68.3 us
  Pallas kernels  62.2 us (91%)
  local copies, waits for them, and re-layouts  6.13 us (9%)
    pallas_call x1, Pallas kernels, on_device(): pl.pallas_call(kernel, out_shape=jax.ShapeDtypeStruct(vectors.shape, F32)...  62.2 us
    unnamed x18, local copies, waits for them, and re-layouts  6.13 us

commit v1 on v0

--- a/solution.py
+++ b/solution.py
@@ -85,6 +85,16 @@
 
 
 def kernel(
+    vec_in,
+    pts_in,
+    noise_in,
+    bases_in,
+    transfer_in,
+    prox_in,
+    src_in,
+    cnt_in,
+    flags_in,
+    out,
     vec,
     pts,
     noise,
@@ -94,7 +104,6 @@
     src,
     cnt,
     flags,
-    out,
     vhl,
     bh,
     bl,
@@ -131,9 +140,28 @@
     gf,
     g2,
     fs,
+    load,
     send,
     recv,
 ):
+    loads = [
+        pltpu.make_async_copy(source, target, load.at[place])
+        for place, (source, target) in enumerate(
+            (
+                (vec_in, vec),
+                (bases_in, bases),
+                (transfer_in, transfer),
+                (pts_in, pts),
+                (prox_in, prox),
+                (noise_in, noise),
+                (src_in, src),
+                (cnt_in, cnt),
+                (flags_in, flags),
+            )
+        )
+    ]
+    for item in loads:
+        item.start()
     edge_of = {2: e2, 3: e3, 4: e4, 5: e5, 6: e6}
     me = lax.axis_index("leaf")
     z, j = me // PLANE, me % PLANE
@@ -168,6 +196,8 @@
             device_id_type=MESH,
         )
 
+    for item in loads:
+        item.wait()
     head, rest = head_and_rest(transfer[...].reshape(2 * RANK, RANK))
     th[...] = head
     tl[...] = rest
@@ -195,7 +225,7 @@
     lane = lax.broadcasted_iota(jnp.int32, (ROWS, 128), 1)
     root_flags = jnp.zeros((ROWS, 128), F32)
     for which in range(3):
-        root_flags = jnp.where(lane == which, flags[6, which].astype(F32), root_flags)
+        root_flags = jnp.where(lane == which, flags[which, 6].astype(F32), root_flags)
     g2[...] = coef2
     for i in range(PLANE):
         sa[i, :, 0:RANK] = g2[ROWS * i : ROWS * (i + 1), :]
@@ -232,10 +262,8 @@
     for axis in range(3):
         side = 2.0 ** ((axis - TOP) / 3.0)
         for place, offset in enumerate((2.0, 3.0)):
-
-            @pl.loop(0, RANK // CHUNK)
-            def _(step):
-                rows = pl.ds(step * CHUNK, CHUNK)
+            for step in range(RANK // CHUNK):
+                rows = slice(step * CHUNK, (step + 1) * CHUNK)
                 squared = None
                 for c in range(3):
                     column = gf[rows, c : c + 1]
@@ -277,18 +305,16 @@
 
     def evaluate(reader, window, slot):
         reader_rows = ppad[:, pl.ds(pl.multiple_of(reader * LEAF, LEAF), LEAF)]
-
-        @pl.loop(0, LEAF // CHUNK)
-        def _(step):
-            rows = pl.ds(step * CHUNK, CHUNK)
+        for step in range(LEAF // CHUNK):
+            rows = slice(step * CHUNK, (step + 1) * CHUNK)
             squared = None
             for c in range(3):
                 delta = cols[window, rows, c : c + 1] - reader_rows[c : c + 1, :]
                 squared = delta * delta if squared is None else squared + delta * delta
             distance = squared * lax.rsqrt(jnp.maximum(squared, 1e-30))
-            u = distance * (ROOT_THREE / SHORT_SCALE)
-            v = distance * (ROOT_THREE / LONG_SCALE)
-            value = (1.0 + u) * jnp.exp2(u * -LOG2_E) + (1.0 + v) * jnp.exp2(v * -LOG2_E)
+            short, long = ROOT_THREE / SHORT_SCALE, ROOT_THREE / LONG_SCALE
+            value = (1.0 + distance * short) * jnp.exp2(distance * (-LOG2_E * short))
+            value = value + (1.0 + distance * long) * jnp.exp2(distance * (-LOG2_E * long))
             head, rest = head_and_rest(value)
             kh[slot, rows, :] = head
             kl[slot, rows, :] = rest
@@ -308,10 +334,19 @@
     for leaf in range(LEAVES):
         columns_of(4 + leaf, ppad[:, leaf * LEAF : (leaf + 1) * LEAF])
 
-    @pl.loop(0, LEAVES)
-    def _(leaf):
-        evaluate(leaf, 4 + leaf, 0)
-        gather_near(leaf, 4 + leaf, 0, NORMAL)
+    def local_pairs(pairs):
+        for place in range(len(pairs) + 1):
+            if place < len(pairs):
+                first, second = pairs[place]
+                evaluate(first, 4 + second, place % 2)
+            if place > 0:
+                first, second = pairs[place - 1]
+                gather_near(first, 4 + second, (place - 1) % 2, NORMAL)
+                if first != second:
+                    gather_near(second, 4 + first, (place - 1) % 2, TRANSPOSED)
+
+    every = [(a, b) for a in range(LEAVES) for b in range(a, LEAVES)]
+    local_pairs(every[:5])
 
     copy(sa.at[pl.ds(0, PLANE - 1)], e2.at[pl.ds(HALO, PLANE - 1)], SEM_A, left).wait_recv()
     edge_copies = []
@@ -356,6 +391,8 @@
     top7[0:HALO] = jnp.zeros((HALO, ROWS, RANK), F32)
     top7[HALO + PLANES :] = jnp.zeros((HALO, ROWS, RANK), F32)
     top8[...] = jnp.zeros_like(top8)
+
+    local_pairs(every[5:])
 
     inside_below = jnp.where(z > 0, 1.0, 0.0)
     inside_above = jnp.where(z < PLANES - 1, 1.0, 0.0)
@@ -448,7 +485,7 @@
 
     def local_field(level, ref, nodes, first_row, target):
         def at(node, which, reader):
-            weight = flags[first_row + reader, which].astype(F32)
+            weight = flags[which, first_row + reader].astype(F32)
             if node < 0:
                 weight = weight * has_left
             if node >= nodes:
@@ -474,19 +511,24 @@
         columns_of(leaf, pside[0, :, lanes])
         columns_of(8 + leaf, pside[1, :, lanes])
 
-    for first in range(LEAVES):
-        for second in range(first + 1, LEAVES):
-            evaluate(first, 4 + second, 0)
-            gather_near(first, 4 + second, 0, NORMAL)
-            gather_near(second, 4 + first, 0, TRANSPOSED)
-
-    @pl.loop(0, 5 * LEAVES)
-    def _(index):
+    def place_of(index):
         reader = index // 5
         step = index % 5
-        window = reader + step + jnp.where(step < 4 - reader, 0, 4)
-        evaluate(reader, window, 0)
-        gather_near(reader, window, 0, NORMAL)
+        return reader, reader + step + jnp.where(step < 4 - reader, 0, 4)
+
+    pairs_count = 5 * LEAVES
+    evaluate(0, 0, 1)
+
+    @pl.loop(0, pairs_count // 2 - 1)
+    def _(step):
+        evaluate(*place_of(2 * step + 1), 0)
+        gather_near(*place_of(2 * step), 1, NORMAL)
+        evaluate(*place_of(2 * step + 2), 1)
+        gather_near(*place_of(2 * step + 1), 0, NORMAL)
+
+    evaluate(*place_of(pairs_count - 1), 0)
+    gather_near(*place_of(pairs_count - 2), 1, NORMAL)
+    gather_near(*place_of(pairs_count - 1), 0, NORMAL)
 
     copy(sb.at[pl.ds(0, PLANE - 1)], rb.at[pl.ds(0, PLANE - 1)], SEM_B, left).wait_recv()
     for i in range(PLANE):
@@ -513,13 +555,22 @@
 
 def on_device(vectors, points, noise, bases, transfer, proxies, near_src, near_count, far_flags):
     vmem = pl.BlockSpec(memory_space=pltpu.VMEM)
-    smem = pl.BlockSpec(memory_space=pltpu.SMEM)
     width = RANK + 128
 
     def buffer(*shape, dtype=F32):
         return pltpu.VMEM(shape, dtype)
 
+    points_count = LEAVES * LEAF
     scratch = [
+        buffer(RHS, points_count),
+        buffer(3, points_count),
+        buffer(1, points_count),
+        buffer(RANK, points_count),
+        buffer(2, RANK, RANK),
+        buffer(3, RANK),
+        pltpu.SMEM((LEAVES, 8), jnp.int32),
+        pltpu.SMEM((LEAVES,), jnp.int32),
+        pltpu.SMEM((3, 2 * LEAVES - 1), jnp.int32),
         buffer(12, 2 * RHS, LEAF, dtype=BF16),
         buffer(RANK, LEAVES * LEAF, dtype=BF16),
         buffer(RANK, LEAVES * LEAF, dtype=BF16),
@@ -556,17 +607,18 @@
         buffer(RANK, 8),
         buffer(RHS, RANK),
         buffer(len(PLANE_LEVELS), RHS, RANK),
+        pltpu.SemaphoreType.DMA((9,)),
         pltpu.SemaphoreType.DMA((SEMS,)),
         pltpu.SemaphoreType.DMA((SEMS,)),
     ]
     return pl.pallas_call(
         kernel,
         out_shape=jax.ShapeDtypeStruct(vectors.shape, F32),
-        in_specs=[vmem] * 6 + [smem] * 3,
+        in_specs=[pl.BlockSpec(memory_space=pltpu.HBM)] * 9,
         out_specs=vmem,
         scratch_shapes=scratch,
         compiler_params=pltpu.CompilerParams(
-            collective_id=0, has_side_effects=True, vmem_limit_bytes=48 * 2**20
+            collective_id=0, has_side_effects=True, vmem_limit_bytes=62 * 2**20
         ),
         cost_estimate=pl.CostEstimate(
             flops=3 * 10**9, bytes_accessed=3 * 10**6, transcendentals=10**7
@@ -580,7 +632,7 @@
         proxies,
         near_src,
         near_count,
-        far_flags,
+        far_flags.T,
     )
 
 

time: 68.7 us -> 36.8 us (0.54)
  the two profiles are of different devices: /device:TPU:1 before, /device:TPU:9 now
where the time goes in v1:
time: 36.8 us; the launch traced here: 36.7 us
  Pallas kernels  35 us (95%)
  local copies, waits for them, and re-layouts  1.67 us (5%)
    pallas_call x1, Pallas kernels, on_device(): pl.pallas_call(kernel, out_shape=jax.ShapeDtypeStruct(vectors.shape, F32)...  35 us
    unnamed x1, local copies, waits for them, and re-layouts  1.67 us

profile of v1, /device:TPU:9, one launch (start us, length us, event | category | flops | bytes accessed | tf_op | source)
XLA Modules:
  0.0 36.7 jit_solution(8807379776162339171)
XLA Ops:
  0.0 35.0 %shard_map.91 = f32[64,1024]{1,0:T(8,128)} custom-call(f32[64,1024]{1,0:T(8,128)} %vec_in.1, f32[3,1024]{1,0:T(4,128)} %pts_in.1, f32[1,1024]{1,0:T(1,128)} %bitcast.2, f32[256,1024]{1,0:T(8,128)} %bases_in.1, f32[2,256,256]{2,1,0:T(8,128)} %transfer_in.1, f32[3,256]{1,0:T(4,128)} %prox_in.1, s32[4,8]{1,0:T(4,128)} %src_in.1, s32[4]{0:T(128)} %cnt_in.1, ...), custom_call_target="tpu_custom_call" | custom-call | flops 3000000000 | bytes 3000000 | tf_op jit(solution)/shard_map/pallas_call | solution.py:614
  35.0 1.7 %copy.11 = f32[64,1024]{1,0:T(8,128)} copy(f32[64,1024]{1,0:T(8,128)} %shard_map.91) | data formatting | bytes 524288

commit v2 on v1

--- a/solution.py
+++ b/solution.py
@@ -28,11 +28,20 @@
 TOP = 10
 HALO = 3
 CHUNK = 32
+LOCAL_FIRST = 4
+LOCAL_CHAIN = 4
+CHAIN_PAIRS = ((0,), (1,), (2,), (3,), (4,))
+FIELD_PAIRS = 4
 
 NORMAL = (((1,), (0,)), ((), ()))
 TRANSPOSED = (((1,), (1,)), ((), ()))
 
 PLANE_LEVELS = (2, 3, 4, 5, 6)
+
+PLANE_ORDER = sorted(
+    range(1, PLANE), key=lambda s: -(min(s // 8, 4 - s // 8) + min(s // 2 % 4, 4 - s // 2 % 4))
+)
+COLUMN_ORDER = (4, 3, 5, 2, 6, 1, 7)
 
 SEM_A, SEM_TOP, SEM_B = 0, 1, 2
 SEM_VEC, SEM_PTS, SEM_RIM0, SEM_RIM1, SEM_EDGE = 3, 5, 7, 9, 11
@@ -160,8 +169,6 @@
             )
         )
     ]
-    for item in loads:
-        item.start()
     edge_of = {2: e2, 3: e3, 4: e4, 5: e5, 6: e6}
     me = lax.axis_index("leaf")
     z, j = me // PLANE, me % PLANE
@@ -175,16 +182,20 @@
     def greet(device):
         pl.semaphore_signal(barrier, inc=1, device_id=(device,), device_id_type=MESH)
 
-    @pl.loop(1, PLANE)
-    def _(step):
-        greet(z * PLANE + (j + step) % PLANE)
-
-    @pl.loop(1, PLANES)
-    def _(step):
-        greet((z + step) % PLANES * PLANE + j)
-
+    def in_plane(step):
+        return lax.rem(j + step, PLANE)
+
+    def in_column(step):
+        return lax.rem(z + step, PLANES)
+
+    for step in PLANE_ORDER:
+        greet(z * PLANE + in_plane(step))
+    for step in COLUMN_ORDER:
+        greet(in_column(step) * PLANE + j)
     greet(left)
     greet(right)
+    for item in loads:
+        item.start()
 
     def copy(source, target, sem, device):
         return pltpu.make_async_remote_copy(
@@ -233,9 +244,8 @@
 
     pl.semaphore_wait(barrier, PLANE - 1 + PLANES - 1 + 2)
 
-    @pl.loop(1, PLANE)
-    def _(step):
-        other = (j + step) % PLANE
+    for step in PLANE_ORDER:
+        other = in_plane(step)
         copy(sa.at[other], e2.at[HALO + j], SEM_A, z * PLANE + other).start()
 
     e2[HALO + j] = sa[j]
@@ -252,9 +262,6 @@
         copy(ex1.at[pl.ds(2, 2)], ex1.at[pl.ds(0, 2)], SEM_RIM1, right),
         copy(ex1.at[pl.ds(2, 2)], ex1.at[pl.ds(4, 2)], SEM_RIM1 + 1, left),
     ]
-    for item in side_copies:
-        item.start()
-
     prox_rows = prox[...]
     prox_cols = jnp.concatenate([prox_rows, jnp.zeros((5, RANK), F32)], axis=0).T
     gf[...] = prox_cols
@@ -295,6 +302,9 @@
             return first, second, even_part, odd_part
         return (first + second + stack(even_part, odd_part, rows)) * (1.0 / 32.0)
 
+    top7[0:HALO] = jnp.zeros((HALO, ROWS, RANK), F32)
+    top7[HALO + PLANES :] = jnp.zeros((HALO, ROWS, RANK), F32)
+    top8[...] = jnp.zeros_like(top8)
     gm[...] = jnp.zeros_like(gm)
     gp[...] = jnp.zeros_like(gp)
     ge[...] = jnp.zeros_like(ge)
@@ -334,21 +344,26 @@
     for leaf in range(LEAVES):
         columns_of(4 + leaf, ppad[:, leaf * LEAF : (leaf + 1) * LEAF])
 
+    def spread(pair, slot):
+        first, second = pair
+        gather_near(first, 4 + second, slot, NORMAL)
+        if first != second:
+            gather_near(second, 4 + first, slot, TRANSPOSED)
+
     def local_pairs(pairs):
         for place in range(len(pairs) + 1):
             if place < len(pairs):
                 first, second = pairs[place]
                 evaluate(first, 4 + second, place % 2)
             if place > 0:
-                first, second = pairs[place - 1]
-                gather_near(first, 4 + second, (place - 1) % 2, NORMAL)
-                if first != second:
-                    gather_near(second, 4 + first, (place - 1) % 2, TRANSPOSED)
+                spread(pairs[place - 1], (place - 1) % 2)
 
     every = [(a, b) for a in range(LEAVES) for b in range(a, LEAVES)]
-    local_pairs(every[:5])
+    local_pairs(every[:LOCAL_FIRST])
 
     copy(sa.at[pl.ds(0, PLANE - 1)], e2.at[pl.ds(HALO, PLANE - 1)], SEM_A, left).wait_recv()
+    for item in side_copies[:4]:
+        item.start()
     edge_copies = []
 
     def send_edges(level):
@@ -367,7 +382,6 @@
             item.start()
             edge_copies.append(item)
 
-    send_edges(2)
     for p in range(PLANE):
         g2[ROWS * p : ROWS * (p + 1), :] = e2[HALO + reversed_bits(p, 5), :, 0:RANK]
     current = g2[...]
@@ -379,20 +393,22 @@
             count = 7 - level
             for p in range(nodes_at(level)):
                 edge_of[level][HALO + reversed_bits(p, count)] = current[ROWS * p : ROWS * (p + 1)]
-            send_edges(level)
+            if level - 3 < LOCAL_CHAIN:
+                pair = every[LOCAL_FIRST + level - 3]
+                evaluate(pair[0], 4 + pair[1], level % 2)
+                spread(pair, level % 2)
     s7[...] = current[0:ROWS]
 
-    @pl.loop(1, PLANES)
-    def _(step):
-        other = (z + step) % PLANES
-        copy(s7, top7.at[HALO + z], SEM_TOP, other * PLANE + j).start()
+    for step in COLUMN_ORDER:
+        copy(s7, top7.at[HALO + z], SEM_TOP, in_column(step) * PLANE + j).start()
+    for level in PLANE_LEVELS:
+        send_edges(level)
+    for item in side_copies[4:]:
+        item.start()
+    middle = every[LOCAL_FIRST + LOCAL_CHAIN :]
+    local_pairs(middle)
 
     top7[HALO + z] = s7[...]
-    top7[0:HALO] = jnp.zeros((HALO, ROWS, RANK), F32)
-    top7[HALO + PLANES :] = jnp.zeros((HALO, ROWS, RANK), F32)
-    top8[...] = jnp.zeros_like(top8)
-
-    local_pairs(every[5:])
 
     inside_below = jnp.where(z > 0, 1.0, 0.0)
     inside_above = jnp.where(z < PLANES - 1, 1.0, 0.0)
@@ -401,7 +417,7 @@
 
     def plane_field(level):
         ref, nodes = edge_of[level], nodes_at(level)
-        count = 7 - level
+        count, slot = 7 - level, level - 2
 
         def at(node):
             value = ref[HALO + node, :, 0:RANK]
@@ -414,19 +430,19 @@
         for p in range(nodes):
             node = reversed_bits(p, count)
             rows = slice(ROWS * p, ROWS * (p + 1))
-            gm[rows, :] = at(node - 2)
-            gp[rows, :] = at(node + 2)
+            gm[slot, rows, :] = at(node - 2)
+            gp[slot, rows, :] = at(node + 2)
             if p < nodes // 2:
-                ge[rows, :] = at(node + 3)
+                ge[slot, rows, :] = at(node + 3)
             else:
                 half = p - nodes // 2
-                go[ROWS * half : ROWS * (half + 1), :] = at(node - 3)
+                go[slot, ROWS * half : ROWS * (half + 1), :] = at(node - 3)
             if level == 2:
                 gf[rows, :] = ref[HALO + node, :, RANK : RANK + 8]
         size = max(ROWS * nodes, 8)
         half_size = max(ROWS * nodes // 2, 8)
-        minus, plus = gm[0:size, :], gp[0:size, :]
-        even, odd = ge[0:half_size, :], go[0:half_size, :]
+        minus, plus = gm[slot, 0:size, :], gp[slot, 0:size, :]
+        even, odd = ge[slot, 0:half_size, :], go[slot, 0:half_size, :]
         if level == 2:
             weights = gf[0:size, :]
             minus = minus * weights[:, 0:1]
@@ -437,6 +453,40 @@
 
     for level in PLANE_LEVELS:
         plane_field(level)
+
+    def take_sides():
+        for item in side_copies[:4]:
+            item.wait_recv()
+        for leaf in range(LEAVES):
+            lanes = slice(leaf * LEAF, (leaf + 1) * LEAF)
+            vhl[leaf] = halves(vside[0, :, lanes])
+            vhl[8 + leaf] = halves(vside[1, :, lanes])
+            columns_of(leaf, pside[0, :, lanes])
+            columns_of(8 + leaf, pside[1, :, lanes])
+
+    def place_of(index):
+        reader = index // 5
+        step = index % 5
+        return reader, reader + step + jnp.where(step < 4 - reader, 0, 4)
+
+    def side_pairs(start, stop):
+        evaluate(*place_of(start), 1)
+
+        @pl.loop(0, (stop - start - 1) // 2)
+        def _(step):
+            index = start + 2 * step
+            evaluate(*place_of(index + 1), 0)
+            gather_near(*place_of(index), 1, NORMAL)
+            evaluate(*place_of(index + 2), 1)
+            gather_near(*place_of(index + 1), 0, NORMAL)
+
+        if (stop - start) % 2 == 0:
+            evaluate(*place_of(stop - 1), 0)
+            gather_near(*place_of(stop - 2), 1, NORMAL)
+            gather_near(*place_of(stop - 1), 0, NORMAL)
+        else:
+            gather_near(*place_of(stop - 1), 1, NORMAL)
+
 
     copy(
         top7.at[pl.ds(HALO, PLANES - 1)], top7.at[pl.ds(HALO, PLANES - 1)], SEM_TOP, left
@@ -449,11 +499,13 @@
 
     def own_field(level, ref, node):
         parity = node % 2
-        gm[0:ROWS, :] = ref[HALO + node - 2]
-        gp[0:ROWS, :] = ref[HALO + node + 2]
-        ge[0:ROWS, :] = ref[jnp.where(parity == 0, HALO + node + 3, HALO + node - 3)]
-        third = ge[0:8, :]
-        first, second, even, odd = field(level, gm[0:8, :], gp[0:8, :], third, third, None)
+        slot = level - 2
+        gm[slot, 0:ROWS, :] = ref[HALO + node - 2]
+        gp[slot, 0:ROWS, :] = ref[HALO + node + 2]
+        ge[slot, 0:ROWS, :] = ref[jnp.where(parity == 0, HALO + node + 3, HALO + node - 3)]
+        third = ge[slot, 0:8, :]
+        minus, plus = gm[slot, 0:8, :], gp[slot, 0:8, :]
+        first, second, even, odd = field(level, minus, plus, third, third, None)
         return (first + second + jnp.where(parity == 0, even, odd)) * (1.0 / 32.0)
 
     def children(parent):
@@ -463,22 +515,28 @@
     down = own_field(8, top8, z // 2)
     both = children(down)
     down = field7 + jnp.where(z % 2 == 0, both[:, :RANK], both[:, RANK:])
+    take_sides()
     for level in (6, 5, 4, 3, 2):
         size = max(ROWS * nodes_at(level), 8)
         both = children(down)
         rows = ROWS * nodes_at(level) // 2
         down = fs[level - 2, 0:size, :] + stack(both[:, :RANK], both[:, RANK:], rows)
+        for pair in CHAIN_PAIRS[6 - level]:
+            evaluate(*place_of(pair), pair % 2)
+            gather_near(*place_of(pair), pair % 2, NORMAL)
     for p in range(PLANE):
         sb[reversed_bits(p, 5)] = down[ROWS * p : ROWS * (p + 1)]
 
-    @pl.loop(1, PLANE)
-    def _(step):
-        other = (j + step) % PLANE
+    for step in PLANE_ORDER:
+        other = in_plane(step)
         copy(sb.at[other], rb.at[j], SEM_B, z * PLANE + other).start()
 
     rb[j] = sb[j]
 
-    for item in side_copies:
+    done = sum(len(group) for group in CHAIN_PAIRS)
+    side_pairs(done, 5 * LEAVES - FIELD_PAIRS)
+    done = 5 * LEAVES - FIELD_PAIRS
+    for item in side_copies[4:]:
         item.wait_recv()
     has_left = jnp.where(me > 0, 1.0, 0.0)
     has_right = jnp.where(me < DEVICES - 1, 1.0, 0.0)
@@ -501,34 +559,19 @@
         for place, n in enumerate(order):
             target[n] = value[RHS * place : RHS * (place + 1)]
 
-    local_field(0, ex0, LEAVES, 0, f0)
-    local_field(1, ex1, LEAVES // 2, LEAVES, f1)
-
-    for leaf in range(LEAVES):
-        lanes = slice(leaf * LEAF, (leaf + 1) * LEAF)
-        vhl[leaf] = halves(vside[0, :, lanes])
-        vhl[8 + leaf] = halves(vside[1, :, lanes])
-        columns_of(leaf, pside[0, :, lanes])
-        columns_of(8 + leaf, pside[1, :, lanes])
-
-    def place_of(index):
-        reader = index // 5
-        step = index % 5
-        return reader, reader + step + jnp.where(step < 4 - reader, 0, 4)
-
-    pairs_count = 5 * LEAVES
-    evaluate(0, 0, 1)
-
-    @pl.loop(0, pairs_count // 2 - 1)
-    def _(step):
-        evaluate(*place_of(2 * step + 1), 0)
-        gather_near(*place_of(2 * step), 1, NORMAL)
-        evaluate(*place_of(2 * step + 2), 1)
-        gather_near(*place_of(2 * step + 1), 0, NORMAL)
-
-    evaluate(*place_of(pairs_count - 1), 0)
-    gather_near(*place_of(pairs_count - 2), 1, NORMAL)
-    gather_near(*place_of(pairs_count - 1), 0, NORMAL)
+    if FIELD_PAIRS:
+        for item in range(FIELD_PAIRS + 1):
+            if item < FIELD_PAIRS:
+                evaluate(*place_of(done + item), item % 2)
+            if item == 0:
+                local_field(0, ex0, LEAVES, 0, f0)
+            if item == 1:
+                local_field(1, ex1, LEAVES // 2, LEAVES, f1)
+            if item > 0:
+                gather_near(*place_of(done + item - 1), (item - 1) % 2, NORMAL)
+    else:
+        local_field(0, ex0, LEAVES, 0, f0)
+        local_field(1, ex1, LEAVES // 2, LEAVES, f1)
 
     copy(sb.at[pl.ds(0, PLANE - 1)], rb.at[pl.ds(0, PLANE - 1)], SEM_B, left).wait_recv()
     for i in range(PLANE):
@@ -600,10 +643,10 @@
     scratch += [
         buffer(PLANES + 2 * HALO, ROWS, RANK),
         buffer(4 + 2 * HALO, ROWS, RANK),
-        buffer(RHS, RANK),
-        buffer(RHS, RANK),
-        buffer(RHS, RANK),
-        buffer(RHS, RANK),
+        buffer(7, RHS, RANK),
+        buffer(7, RHS, RANK),
+        buffer(7, RHS, RANK),
+        buffer(7, RHS, RANK),
         buffer(RANK, 8),
         buffer(RHS, RANK),
         buffer(len(PLANE_LEVELS), RHS, RANK),

time: 36.8 us -> 33.2 us (0.902)
  the two profiles are of different devices: /device:TPU:9 before, /device:TPU:1 now
where the time goes in v2:
time: 33.2 us; the launch traced here: 33.1 us
  Pallas kernels  31.4 us (95%)
  local copies, waits for them, and re-layouts  1.67 us (5%)
    pallas_call x1, Pallas kernels, on_device(): pl.pallas_call(kernel, out_shape=jax.ShapeDtypeStruct(vectors.shape, F32)...  31.4 us
    unnamed x1, local copies, waits for them, and re-layouts  1.67 us

profile of v2, /device:TPU:1, one launch (start us, length us, event | category | flops | bytes accessed | tf_op | source)
XLA Modules:
  0.0 33.1 jit_solution(10116391540397384683)
XLA Ops:
  0.0 31.4 %shard_map.91 = f32[64,1024]{1,0:T(8,128)} custom-call(f32[64,1024]{1,0:T(8,128)} %vec_in.1, f32[3,1024]{1,0:T(4,128)} %pts_in.1, f32[1,1024]{1,0:T(1,128)} %bitcast.2, f32[256,1024]{1,0:T(8,128)} %bases_in.1, f32[2,256,256]{2,1,0:T(8,128)} %transfer_in.1, f32[3,256]{1,0:T(4,128)} %prox_in.1, s32[4,8]{1,0:T(4,128)} %src_in.1, s32[4]{0:T(128)} %cnt_in.1, ...), custom_call_target="tpu_custom_call" | custom-call | flops 3000000000 | bytes 3000000 | tf_op jit(solution)/shard_map/pallas_call | solution.py:657
  31.4 1.7 %copy.11 = f32[64,1024]{1,0:T(8,128)} copy(f32[64,1024]{1,0:T(8,128)} %shard_map.91) | data formatting | bytes 524288

commit v3 on v2

--- a/solution.py
+++ b/solution.py
@@ -1,6 +1,3 @@
-import functools
-import math
-
 import jax
 import jax.numpy as jnp
 from jax import lax
@@ -31,7 +28,6 @@
 LOCAL_FIRST = 4
 LOCAL_CHAIN = 4
 CHAIN_PAIRS = ((0,), (1,), (2,), (3,), (4,))
-FIELD_PAIRS = 4
 
 NORMAL = (((1,), (0,)), ((), ()))
 TRANSPOSED = (((1,), (1,)), ((), ()))
@@ -44,7 +40,7 @@
 COLUMN_ORDER = (4, 3, 5, 2, 6, 1, 7)
 
 SEM_A, SEM_TOP, SEM_B = 0, 1, 2
-SEM_VEC, SEM_PTS, SEM_RIM0, SEM_RIM1, SEM_EDGE = 3, 5, 7, 9, 11
+SEM_VEC, SEM_PTS, SEM_RIM0, SEM_RIM1, SEM_FAR, SEM_EDGE = 3, 5, 7, 9, 11, 13
 SEMS = SEM_EDGE + 2 * len(PLANE_LEVELS)
 
 
@@ -252,11 +248,18 @@
 
     ppad[...] = jnp.zeros_like(ppad)
     ppad[0:3, :] = pts[...]
+
+    def side_copy(side, first, sem, device):
+        lanes = pl.ds(first * LEAF, 2 * LEAF)
+        return copy(vec.at[:, lanes], vside.at[side, :, lanes], sem, device)
+
     side_copies = [
         copy(ppad, pside.at[0], SEM_PTS, right),
         copy(ppad, pside.at[1], SEM_PTS + 1, left),
-        copy(vec, vside.at[0], SEM_VEC, right),
-        copy(vec, vside.at[1], SEM_VEC + 1, left),
+        side_copy(0, 2, SEM_VEC, right),
+        side_copy(1, 0, SEM_VEC + 1, left),
+        side_copy(0, 0, SEM_FAR, right),
+        side_copy(1, 2, SEM_FAR + 1, left),
         copy(ex0.at[pl.ds(4, 2)], ex0.at[pl.ds(0, 2)], SEM_RIM0, right),
         copy(ex0.at[pl.ds(2, 2)], ex0.at[pl.ds(6, 2)], SEM_RIM0 + 1, left),
         copy(ex1.at[pl.ds(2, 2)], ex1.at[pl.ds(0, 2)], SEM_RIM1, right),
@@ -362,8 +365,6 @@
     local_pairs(every[:LOCAL_FIRST])
 
     copy(sa.at[pl.ds(0, PLANE - 1)], e2.at[pl.ds(HALO, PLANE - 1)], SEM_A, left).wait_recv()
-    for item in side_copies[:4]:
-        item.start()
     edge_copies = []
 
     def send_edges(level):
@@ -382,6 +383,9 @@
             item.start()
             edge_copies.append(item)
 
+    send_edges(2)
+    for item in side_copies[:4]:
+        item.start()
     for p in range(PLANE):
         g2[ROWS * p : ROWS * (p + 1), :] = e2[HALO + reversed_bits(p, 5), :, 0:RANK]
     current = g2[...]
@@ -401,7 +405,7 @@
 
     for step in COLUMN_ORDER:
         copy(s7, top7.at[HALO + z], SEM_TOP, in_column(step) * PLANE + j).start()
-    for level in PLANE_LEVELS:
+    for level in PLANE_LEVELS[1:]:
         send_edges(level)
     for item in side_copies[4:]:
         item.start()
@@ -412,8 +416,6 @@
 
     inside_below = jnp.where(z > 0, 1.0, 0.0)
     inside_above = jnp.where(z < PLANES - 1, 1.0, 0.0)
-    for item in edge_copies:
-        item.wait_recv()
 
     def plane_field(level):
         ref, nodes = edge_of[level], nodes_at(level)
@@ -451,23 +453,29 @@
             odd = odd * weights[half_size:, 2:3]
         fs[level - 2, 0:size, :] = field(level, minus, plus, even, odd, ROWS * nodes // 2)
 
-    for level in PLANE_LEVELS:
+    for item in edge_copies[:2]:
+        item.wait_recv()
+    plane_field(2)
+    for item in edge_copies[2:]:
+        item.wait_recv()
+    for level in PLANE_LEVELS[1:]:
         plane_field(level)
 
-    def take_sides():
-        for item in side_copies[:4]:
+    def take_sides(items, side_leaves):
+        for item in items:
             item.wait_recv()
-        for leaf in range(LEAVES):
+        for side, leaf in side_leaves:
             lanes = slice(leaf * LEAF, (leaf + 1) * LEAF)
-            vhl[leaf] = halves(vside[0, :, lanes])
-            vhl[8 + leaf] = halves(vside[1, :, lanes])
-            columns_of(leaf, pside[0, :, lanes])
-            columns_of(8 + leaf, pside[1, :, lanes])
+            vhl[8 * side + leaf] = halves(vside[side, :, lanes])
+            columns_of(8 * side + leaf, pside[side, :, lanes])
 
     def place_of(index):
-        reader = index // 5
-        step = index % 5
-        return reader, reader + step + jnp.where(step < 4 - reader, 0, 4)
+        if isinstance(index, int):
+            return (index // 2, 3 - index % 2) if index < 7 else (3 - (index - 7) // 2, 8 + (index - 7) % 2)
+        on_left = index < 7
+        place = jnp.where(on_left, index, index - 7)
+        half, odd = lax.div(place, 2), lax.rem(place, 2)
+        return jnp.where(on_left, half, 3 - half), jnp.where(on_left, 3 - odd, 8 + odd)
 
     def side_pairs(start, stop):
         evaluate(*place_of(start), 1)
@@ -515,7 +523,7 @@
     down = own_field(8, top8, z // 2)
     both = children(down)
     down = field7 + jnp.where(z % 2 == 0, both[:, :RANK], both[:, RANK:])
-    take_sides()
+    take_sides(side_copies[:4], ((0, 2), (0, 3), (1, 0), (1, 1)))
     for level in (6, 5, 4, 3, 2):
         size = max(ROWS * nodes_at(level), 8)
         both = children(down)
@@ -533,10 +541,9 @@
 
     rb[j] = sb[j]
 
-    done = sum(len(group) for group in CHAIN_PAIRS)
-    side_pairs(done, 5 * LEAVES - FIELD_PAIRS)
-    done = 5 * LEAVES - FIELD_PAIRS
-    for item in side_copies[4:]:
+    side_pairs(sum(len(group) for group in CHAIN_PAIRS), 14)
+    take_sides(side_copies[4:6], ((0, 0), (0, 1), (1, 2), (1, 3)))
+    for item in side_copies[6:]:
         item.wait_recv()
     has_left = jnp.where(me > 0, 1.0, 0.0)
     has_right = jnp.where(me < DEVICES - 1, 1.0, 0.0)
@@ -559,19 +566,16 @@
         for place, n in enumerate(order):
             target[n] = value[RHS * place : RHS * (place + 1)]
 
-    if FIELD_PAIRS:
-        for item in range(FIELD_PAIRS + 1):
-            if item < FIELD_PAIRS:
-                evaluate(*place_of(done + item), item % 2)
-            if item == 0:
-                local_field(0, ex0, LEAVES, 0, f0)
-            if item == 1:
-                local_field(1, ex1, LEAVES // 2, LEAVES, f1)
-            if item > 0:
-                gather_near(*place_of(done + item - 1), (item - 1) % 2, NORMAL)
-    else:
-        local_field(0, ex0, LEAVES, 0, f0)
-        local_field(1, ex1, LEAVES // 2, LEAVES, f1)
+    last = ((0, 0), (0, 1), (1, 1), (3, 11), (3, 10), (2, 10))
+    for item in range(len(last) + 1):
+        if item < len(last):
+            evaluate(*last[item], item % 2)
+        if item == 0:
+            local_field(0, ex0, LEAVES, 0, f0)
+        if item == 1:
+            local_field(1, ex1, LEAVES // 2, LEAVES, f1)
+        if item > 0:
+            gather_near(*last[item - 1], (item - 1) % 2, NORMAL)
 
     copy(sb.at[pl.ds(0, PLANE - 1)], rb.at[pl.ds(0, PLANE - 1)], SEM_B, left).wait_recv()
     for i in range(PLANE):

time: 33.2 us -> 32.9 us (level)
  no operation moved by 1% of the time
where the time goes in v3:
time: 32.9 us; the launch traced here: 32.8 us
  Pallas kernels  31.1 us (95%)
  local copies, waits for them, and re-layouts  1.67 us (5%)
    pallas_call x1, Pallas kernels, on_device(): pl.pallas_call(kernel, out_shape=jax.ShapeDtypeStruct(vectors.shape, F32)...  31.1 us
    unnamed x1, local copies, waits for them, and re-layouts  1.67 us

profile of v3, /device:TPU:1, one launch (start us, length us, event | category | flops | bytes accessed | tf_op | source)
XLA Modules:
  0.0 32.8 jit_solution(10546353760675717103)
XLA Ops:
  0.0 31.1 %shard_map.91 = f32[64,1024]{1,0:T(8,128)} custom-call(f32[64,1024]{1,0:T(8,128)} %vec_in.1, f32[3,1024]{1,0:T(4,128)} %pts_in.1, f32[1,1024]{1,0:T(1,128)} %bitcast.2, f32[256,1024]{1,0:T(8,128)} %bases_in.1, f32[2,256,256]{2,1,0:T(8,128)} %transfer_in.1, f32[3,256]{1,0:T(4,128)} %prox_in.1, s32[4,8]{1,0:T(4,128)} %src_in.1, s32[4]{0:T(128)} %cnt_in.1, ...), custom_call_target="tpu_custom_call" | custom-call | flops 3000000000 | bytes 3000000 | tf_op jit(solution)/shard_map/pallas_call | solution.py:661
  31.1 1.7 %copy.11 = f32[64,1024]{1,0:T(8,128)} copy(f32[64,1024]{1,0:T(8,128)} %shard_map.91) | data formatting | bytes 524288

commit v4 on v3

--- a/solution.py
+++ b/solution.py
@@ -100,6 +100,8 @@
     cnt_in,
     flags_in,
     out,
+    result,
+    store,
     vec,
     pts,
     noise,
@@ -583,14 +585,25 @@
     both = children(g2[...])
     down1 = jnp.concatenate([f1[0] + both[:, :RANK], f1[1] + both[:, RANK:]], axis=0)
     both = children(down1)
+    stores = []
     for leaf in range(LEAVES):
         lanes = slice(leaf * LEAF, (leaf + 1) * LEAF)
         part = both[RHS * (leaf // 2) : RHS * (leaf // 2 + 1)]
         part = part[:, RANK * (leaf % 2) : RANK * (leaf % 2 + 1)]
         far = mul(halves(f0[leaf] + part), bh[:, lanes], bl[:, lanes])
         own = noise[:, lanes] * vec[:, lanes]
-        out[:, lanes] = own + far + near[leaf] * (1.0 / 32.0)
-
+        result[:, lanes] = own + far + near[leaf] * (1.0 / 32.0)
+        stores.append(
+            pltpu.make_async_copy(
+                result.at[:, pl.ds(leaf * LEAF, LEAF)],
+                out.at[:, pl.ds(leaf * LEAF, LEAF)],
+                store.at[leaf],
+            )
+        )
+        stores[-1].start()
+
+    for item in stores:
+        item.wait()
     copy(sa.at[pl.ds(0, PLANE - 1)], e2.at[pl.ds(HALO, PLANE - 1)], SEM_A, left).wait_send()
     copy(sb.at[pl.ds(0, PLANE - 1)], rb.at[pl.ds(0, PLANE - 1)], SEM_B, left).wait_send()
     copy(
@@ -601,7 +614,6 @@
 
 
 def on_device(vectors, points, noise, bases, transfer, proxies, near_src, near_count, far_flags):
-    vmem = pl.BlockSpec(memory_space=pltpu.VMEM)
     width = RANK + 128
 
     def buffer(*shape, dtype=F32):
@@ -609,6 +621,8 @@
 
     points_count = LEAVES * LEAF
     scratch = [
+        buffer(RHS, points_count),
+        pltpu.SemaphoreType.DMA((LEAVES,)),
         buffer(RHS, points_count),
         buffer(3, points_count),
         buffer(1, points_count),
@@ -662,7 +676,7 @@
         kernel,
         out_shape=jax.ShapeDtypeStruct(vectors.shape, F32),
         in_specs=[pl.BlockSpec(memory_space=pltpu.HBM)] * 9,
-        out_specs=vmem,
+        out_specs=pl.BlockSpec(memory_space=pltpu.HBM),
         scratch_shapes=scratch,
         compiler_params=pltpu.CompilerParams(
             collective_id=0, has_side_effects=True, vmem_limit_bytes=62 * 2**20

time: 32.9 us -> 32.9 us (level)
  no operation moved by 1% of the time
where the time goes in v4:
time: 32.9 us; the launch traced here: 32.8 us
  Pallas kernels  31.1 us (95%)
  local copies, waits for them, and re-layouts  1.67 us (5%)
    pallas_call x1, Pallas kernels, on_device(): pl.pallas_call(kernel, out_shape=jax.ShapeDtypeStruct(vectors.shape, F32)...  31.1 us
    unnamed x1, local copies, waits for them, and re-layouts  1.67 us

profile of v4, /device:TPU:1, one launch (start us, length us, event | category | flops | bytes accessed | tf_op | source)
XLA Modules:
  0.0 32.8 jit_solution(16760389371871857455)
XLA Ops:
  0.0 31.1 %shard_map.91 = f32[64,1024]{1,0:T(8,128)} custom-call(f32[64,1024]{1,0:T(8,128)} %vec_in.1, f32[3,1024]{1,0:T(4,128)} %pts_in.1, f32[1,1024]{1,0:T(1,128)} %bitcast.2, f32[256,1024]{1,0:T(8,128)} %bases_in.1, f32[2,256,256]{2,1,0:T(8,128)} %transfer_in.1, f32[3,256]{1,0:T(4,128)} %prox_in.1, s32[4,8]{1,0:T(4,128)} %src_in.1, s32[4]{0:T(128)} %cnt_in.1, ...), custom_call_target="tpu_custom_call" | custom-call | flops 3000000000 | bytes 3000000 | tf_op jit(solution)/shard_map/pallas_call | solution.py:675
  31.1 1.7 %copy.11 = f32[64,1024]{1,0:T(8,128)} copy(f32[64,1024]{1,0:T(8,128)} %shard_map.91) | data formatting | bytes 524288
